TPU v7x, 32 devices: a whole 2x2x4 slice. The times are simulated.
32 devices in a mesh: samples: 2 (over x), brick: 16 (over z, y, core).
Axes of the slice: x: 2, y: 2, z: 4, core: 2. Of those that a mesh axis runs over, the one named last changes fastest.
Arguments:
- source: float32 [128, 128, 256], P(('samples', 'brick')), parts along dimension 0, may hold values from -6 to 6
- guess: float32 [128, 128, 256], P(('samples', 'brick')), parts along dimension 0, may hold values from -6 to 6
- log_perm: float32 [128, 128, 256], P(('samples', 'brick')), parts along dimension 0, may hold values from -3 to 3
- owner: int32 [16], replicated, may hold values from 0 to 15, each once
Outputs:
- corrected: float32 [128, 128, 256], P(('samples', 'brick')), parts along dimension 0
- coarse_held: float32 [32, 2048], P(('samples', 'brick')), parts along dimension 0
There are 2 independent parts, one for each index of `samples`. A program takes and returns all parts, laid end to end along the dimension named above; an argument that names none is the same for every part. Nothing has to cross between parts.
Inputs may be any that keep to these rules, and one draw needn't show every extreme that they name: `owner`: each brick index appears exactly once.
All inputs are finite; a program needn't handle non-finite values.
Results may differ from a plain program's by a relative error of at most 0.00005.
Values sent between devices are 32-bit elements; how exact they have to be, the bound alone decides.
A program may use at most 64 MiB of HBM per device.

v0:
```python
import jax
import jax.numpy as jnp
from jax import lax
from jax.sharding import PartitionSpec as P

NU = 2
SWEEPS = 8
relax_weight = 0.8


def with_halo(block, sides, width):
    for axis, dim in sides:
        count = lax.axis_size(axis)
        forward = [(i, i + 1) for i in range(count - 1)]
        backward = [(target, source) for source, target in forward]
        low = lax.ppermute(
            lax.slice_in_dim(block, block.shape[dim] - width, None, axis=dim), axis, forward
        )
        high = lax.ppermute(lax.slice_in_dim(block, 0, width, axis=dim), axis, backward)
        block = jnp.concatenate([low, block, high], axis=dim)
    return block


def prolong_matrix(n_fine):
    fine_idx = jnp.arange(n_fine)[:, None]
    coarse_idx = jnp.arange(n_fine // 4)[None, :]
    base = fine_idx // 4
    offset = fine_idx % 4
    weight_own = jnp.where((offset == 0) | (offset == 3), 0.625, 0.875).astype(jnp.float32)
    side = jnp.where(offset < 2, -1, 1)
    own = jnp.where(coarse_idx == base, weight_own, 0.0)
    other = jnp.where(coarse_idx == base + side, 1.0 - weight_own, 0.0)
    return own + other


def local_prolong(planes):
    fine_idx = jnp.arange(planes)[:, None]
    coarse_idx = jnp.arange(planes // 4 + 2)[None, :]
    base = fine_idx // 4 + 1
    offset = fine_idx % 4
    weight_own = jnp.where((offset == 0) | (offset == 3), 0.625, 0.875).astype(jnp.float32)
    side = jnp.where(offset < 2, -1, 1)
    own = jnp.where(coarse_idx == base, weight_own, 0.0)
    other = jnp.where(coarse_idx == base + side, 1.0 - weight_own, 0.0)
    return own + other


def stencil(u_ext, k_ext):
    padded = jnp.pad(u_ext, ((0, 0), (1, 1), (1, 1)))
    kpad = jnp.pad(k_ext, ((0, 0), (1, 1), (1, 1)))
    center = padded[1:-1, 1:-1, 1:-1]
    kcen = kpad[1:-1, 1:-1, 1:-1]
    pairs = [
        (padded[:-2, 1:-1, 1:-1], kpad[:-2, 1:-1, 1:-1]),
        (padded[2:, 1:-1, 1:-1], kpad[2:, 1:-1, 1:-1]),
        (padded[1:-1, :-2, 1:-1], kpad[1:-1, :-2, 1:-1]),
        (padded[1:-1, 2:, 1:-1], kpad[1:-1, 2:, 1:-1]),
        (padded[1:-1, 1:-1, :-2], kpad[1:-1, 1:-1, :-2]),
        (padded[1:-1, 1:-1, 2:], kpad[1:-1, 1:-1, 2:]),
    ]
    diagonal = jnp.zeros_like(center)
    nearby = jnp.zeros_like(center)
    for value, kval in pairs:
        face = 0.5 * (kcen + kval)
        diagonal = diagonal + face
        nearby = nearby + face * value
    return (diagonal * center - nearby, diagonal)


def coarse_apply(field, coeff, zcount):
    columns = field.shape[1]
    zpos = jnp.arange(columns) % zcount
    low_ok = (zpos > 0)[None, :]
    high_ok = (zpos < zcount - 1)[None, :]

    def rows_down(a):
        return jnp.pad(a[:-1], ((1, 0), (0, 0)))

    def rows_up(a):
        return jnp.pad(a[1:], ((0, 1), (0, 0)))

    def cols_down(a, width):
        return jnp.pad(a[:, :-width], ((0, 0), (width, 0)))

    def cols_up(a, width):
        return jnp.pad(a[:, width:], ((0, 0), (0, width)))

    pairs = [
        (rows_down(field), rows_down(coeff)),
        (rows_up(field), rows_up(coeff)),
        (cols_down(field, zcount), cols_down(coeff, zcount)),
        (cols_up(field, zcount), cols_up(coeff, zcount)),
        (jnp.where(low_ok, cols_down(field, 1), 0.0), jnp.where(low_ok, cols_down(coeff, 1), 0.0)),
        (jnp.where(high_ok, cols_up(field, 1), 0.0), jnp.where(high_ok, cols_up(coeff, 1), 0.0)),
    ]
    diagonal = jnp.zeros_like(field)
    nearby = jnp.zeros_like(field)
    for value, kval in pairs:
        face = 0.5 * (coeff + kval)
        diagonal = diagonal + face
        nearby = nearby + face * value
    return (diagonal * field - nearby, diagonal)


def faces(field):
    return with_halo(field, (("brick", 0),), 1)


def local(source, guess, log_perm, owner):
    hp = lax.Precision.HIGHEST
    planes, ny_local, nz_local = source.shape
    cpd = planes // 4
    cyc = ny_local // 4
    czc = nz_local // 4
    cells = cyc * czc
    count = lax.axis_size("brick")
    device = lax.axis_index("brick")
    perm = jnp.exp(log_perm)
    k_ext = with_halo(perm, (("brick", 0),), 1)
    smooth = guess
    for sweep in range(NU):
        image, diagonal = stencil(faces(smooth), k_ext)
        smooth = smooth + relax_weight * (source - image) / diagonal
    image, diagonal = stencil(faces(smooth), k_ext)
    resid = source - image
    py = prolong_matrix(ny_local)
    pz = prolong_matrix(nz_local)
    p_local = local_prolong(planes)
    step_one = jnp.einsum("xyz,yY->xYz", resid, py, precision=hp)
    step_two = jnp.einsum("xYz,zZ->xYZ", step_one, pz, precision=hp)
    partial_value = jnp.einsum("xYZ,xj->jYZ", step_two, p_local, precision=hp) * (1.0 / 64.0)
    partial_value = partial_value.reshape(cpd + 2, cells)
    coarse_own = perm.reshape(cpd, 4, cyc, 4, czc, 4).sum(axis=(1, 3, 5)) * (1.0 / 64.0)
    coarse_own = coarse_own.reshape(cpd, cells)
    middle = partial_value[1 : cpd + 1]
    has_prev = device > 0
    has_next = device < count - 1
    filler = jnp.zeros((cpd - 1, cells), jnp.float32)
    lower_part = jnp.concatenate([filler, partial_value[0:1]], axis=0)
    upper_part = jnp.concatenate([partial_value[cpd + 1 :], filler], axis=0)
    block_ids = jnp.arange(count)[:, None, None]
    self_dest = jnp.take(owner, device)
    prev_dest = jnp.take(owner, jnp.clip(device - 1, 0, count - 1))
    next_dest = jnp.take(owner, jnp.clip(device + 1, 0, count - 1))
    buffer = jnp.where(block_ids == self_dest, middle[None], 0.0)
    buffer = buffer + jnp.where((block_ids == prev_dest) & has_prev, lower_part[None], 0.0)
    buffer = buffer + jnp.where((block_ids == next_dest) & has_next, upper_part[None], 0.0)
    held_rhs = lax.psum_scatter(buffer, "brick", scatter_dimension=0, tiled=True)
    gathered_rhs, coarse_perm = (
        lax.all_gather(held_rhs.reshape(cpd, cells), "brick", axis=0, tiled=True),
        lax.all_gather(coarse_own, "brick", axis=0, tiled=True),
    )
    coarse_rhs = jnp.take(gathered_rhs.reshape(count, cpd, cells), owner, axis=0).reshape(
        count * cpd, cells
    )
    coarse = jnp.zeros_like(coarse_rhs)
    for sweep in range(SWEEPS):
        image, diagonal = coarse_apply(coarse, coarse_perm, czc)
        coarse = coarse + relax_weight * (coarse_rhs - image * (1.0 / 16.0)) / (
            diagonal * (1.0 / 16.0)
        )
    coarse_pad = jnp.pad(coarse, ((1, 1), (0, 0)))
    near_planes = lax.dynamic_slice_in_dim(coarse_pad, device * cpd, cpd + 2, 0).reshape(
        cpd + 2, cyc, czc
    )
    back_one = jnp.einsum("jYZ,xj->xYZ", near_planes, p_local, precision=hp)
    back_two = jnp.einsum("xYZ,yY->xyZ", back_one, py, precision=hp)
    correction = jnp.einsum("xyZ,zZ->xyz", back_two, pz, precision=hp)
    corrected = smooth + correction
    my_block = jnp.sum(jnp.where(owner == device, jnp.arange(count), 0))
    coarse_held = lax.dynamic_slice_in_dim(coarse, my_block * cpd, cpd, 0)
    return (corrected, coarse_held)


def solution(mesh):
    placed = (
        P(("samples", "brick"), None, None),
        P(("samples", "brick"), None, None),
        P(("samples", "brick"), None, None),
        P(),
    )
    return jax.shard_map(
        local,
        mesh=mesh,
        in_specs=placed,
        out_specs=(P(("samples", "brick"), None, None), P(("samples", "brick"), None)),
        check_vma=False,
    )
```

profile of v0, /device:TPU:0, one launch (start us, length us, event | category | flops | bytes accessed | tf_op | source)
XLA Modules:
  0.0 212.1 jit_solution(589605700976618355)
XLA Ops:
  7.2 1.2 exponential_reduce_fusion
  8.4 2.4 %collective-permute-start = (f32[1,128,256]{2,1,0:T(8,128)S(1)}, f32[1,128,256]{2,1,0:T(8,128)S(1)}, u32[]{:S(2)}, u32[]{:S(2)}) collective-permute-start(f32[1,128,256]{2,1,0:T(8,128)S(1)} %get-tuple-element.52), channel_id=1, source_target_pairs={{0,1},{1,2},{2,3},{3,4},{4,5},{5,6},{6,7},{7,8},{8,9},{9,10},{10,1... | collective-permute-start | bytes 393224 | tf_op jit(solution)/shard_map/ppermute | solution.py:16
  10.8 1.3 collective-permute-start.1
  12.1 5.8 %collective-permute-start.2 = (f32[1,128,256]{2,1,0:T(8,128)S(1)}, f32[1,128,256]{2,1,0:T(8,128)}, u32[]{:S(2)}, u32[]{:S(2)}) collective-permute-start(f32[1,128,256]{2,1,0:T(8,128)S(1)} %get-tuple-element.53), channel_id=1, source_target_pairs={{0,1},{1,2},{2,3},{3,4},{4,5},{5,6},{6,7},{7,8},{8,9},{9,10},{10,1... | collective-permute-start | bytes 393224 | tf_op jit(solution)/shard_map/ppermute | solution.py:16
  18.0 1.3 collective-permute-start.3
  19.3 5.7 %reduce_sum.26 = f32[32,4,64,4]{3,2,1,0:T(8,128)} reshape(f32[128,256]{1,0:T(8,128)S(1)} %get-tuple-element.45) | data formatting | bytes 262144 | tf_op jit(solution)/shard_map/reduce_sum | solution.py:133
  25.0 2.5 %reduce_sum.27 = f32[32,64]{1,0:T(8,128)S(1)} reduce(f32[32,4,64,4]{3,2,1,0:T(8,128)} %reduce_sum.26, f32[]{:T(128)} %constant.184.clone.1), dimensions={1,3}, to_apply=%region_2.3 | reduce | flops 30720 | bytes 139268 | tf_op jit(solution)/shard_map/reduce_sum | solution.py:133
  27.6 23.8 %all-gather.1 = f32[16,1,2048]{2,1,0:T(1,128)S(1)} all-gather(f32[1,1,2048]{2,1,0:T(1,128)S(1)} %reshape.582), channel_id=1, replica_groups=mesh['samples'=2,'brick'=16] {'brick'}, dimensions={0}, use_global_device_ids=true | all-gather | bytes 139264 | tf_op jit(solution)/shard_map/all_gather | solution.py:151
  52.4 0.8 fusion.149
  53.8 0.8 copy_bitcast_fusion
  57.8 1.3 select_maximum_fusion.6
  59.8 1.3 select_maximum_fusion.4
  61.2 2.2 %fusion.37 = f32[4,128,256]{2,1,0:T(8,128)S(1)} fusion(f32[4,128,256]{2,1,0:T(8,128)S(1)} %copy-done, f32[4,128,256]{2,1,0:T(8,128)S(1)} %copy-done.1, f32[6,130,258]{2,1,0:T(8,128)S(1)} %select_maximum_fusion.4, f32[1,128,256]{2,1,0:T(8,128)} %copy-done.11, f32[1,128,256]{2,1,0:T(8,128)} %collective-permute-done.2, ...), kind=kLoop, calls=%fused_computation.61 | loop fusion | flops 4980736 | bytes 6815744 | tf_op jit(solution)/shard_map/add | solution.py:123
  63.4 2.3 %collective-permute-start.4 = (f32[1,128,256]{2,1,0:T(8,128)S(1)}, f32[1,128,256]{2,1,0:T(8,128)S(1)}, u32[]{:S(2)}, u32[]{:S(2)}) collective-permute-start(f32[1,128,256]{2,1,0:T(8,128)S(1)} %get-tuple-element.49), channel_id=1, source_target_pairs={{0,1},{1,2},{2,3},{3,4},{4,5},{5,6},{6,7},{7,8},{8,9},{9,10},{10,1... | collective-permute-start | bytes 393224 | tf_op jit(solution)/shard_map/ppermute | solution.py:16
  65.6 1.3 collective-permute-start.5
  67.5 1.3 collective-permute-done.5
  70.0 2.2 %fusion.25 = f32[4,128,256]{2,1,0:T(8,128)S(1)} fusion(f32[4,128,256]{2,1,0:T(8,128)S(1)} %fusion.37, f32[4,128,256]{2,1,0:T(8,128)S(1)} %copy-done.1, f32[6,130,258]{2,1,0:T(8,128)S(1)} %select_maximum_fusion.2, f32[1,128,256]{2,1,0:T(8,128)} %copy-done.13, f32[1,128,256]{2,1,0:T(8,128)} %copy-done.12, f32[4,128,256]{2,1,0:T(8,128)S(1)} %get-tuple-element.46, ...), kind=kLoop, calls=%fused_computation.43 | loop fusion | flops 4980736 | bytes 6815744 | tf_op jit(solution)/shard_map/add | solution.py:123
  72.9 5.0 %collective-permute-start.6 = (f32[1,128,256]{2,1,0:T(8,128)}, f32[1,128,256]{2,1,0:T(8,128)S(1)}, u32[]{:S(2)}, u32[]{:S(2)}) collective-permute-start(f32[1,128,256]{2,1,0:T(8,128)} %get-tuple-element.47), channel_id=1, source_target_pairs={{0,1},{1,2},{2,3},{3,4},{4,5},{5,6},{6,7},{7,8},{8,9},{9,10},{10,1... | collective-permute-start | bytes 393224 | tf_op jit(solution)/shard_map/ppermute | solution.py:16
  77.9 1.3 collective-permute-start.7
  82.3 2.4 %convolution_bitcast_fusion = f32[4,32,256]{2,1,0:T(8,128)S(1)} fusion(f32[4,128,256]{2,1,0:T(8,128)S(1)} %copy-done.1, f32[6,130,258]{2,1,0:T(8,128)S(1)} %select_maximum_fusion, f32[1,128,256]{2,1,0:T(8,128)S(1)} %collective-permute-done.7, f32[4,128,256]{2,1,0:T(8,128)S(1)} %fusion.25, f32[1,128,256]{2,1,0:T(8,128)S(1)} %collective-permute-done.6, ...), kind=kOutput, calls=%fused_computation.17 | convolution fusion | flops 54939648 | bytes 6424576 | tf_op jit(solution)/shard_map/xyz,yY->xYz/dot_general | solution.py:129
  86.6 87.5 %all-reduce.62.cloned.1.call-done = f32[16,1,2048]{2,0,1:T(8,128)} async-done(((f32[16,1,2048]{2,0,1:T(8,128)}), f32[16,1,2048]{2,0,1:T(8,128)}) %all-reduce.62.cloned.1.call-update) | async-done | bytes 131088
  174.0 1.4 dynamic-slice_bitcast_fusion
  175.4 22.6 %all-gather = f32[16,1,2048]{2,1,0:T(1,128)S(1)} all-gather(f32[1,1,2048]{2,1,0:T(1,128)S(1)} %dynamic-slice_bitcast_fusion), channel_id=2, replica_groups=mesh['samples'=2,'brick'=16] {'brick'}, dimensions={0}, use_global_device_ids=true | all-gather | bytes 139264 | tf_op jit(solution)/shard_map/all_gather | solution.py:150
  203.2 1.4 convolution_add_fusion
  (116 shorter events, 14.5 us)
Async XLA Ops:
  7.2 4.9 %copy-start = (f32[4,128,256]{2,1,0:T(8,128)S(1)}, f32[4,128,256]{2,1,0:T(8,128)}, u32[]{:S(2)}) copy-start(f32[4,128,256]{2,1,0:T(8,128)} %param.5) | copy-start | bytes 1572868
  7.2 166.9 %all-reduce.62.cloned.1.call-start = ((), (), s32[]{:S(2)}) async-start(), calls=%async_computation | async-start | bytes 262144
  8.4 48.7 %collective-permute-start = (f32[1,128,256]{2,1,0:T(8,128)S(1)}, f32[1,128,256]{2,1,0:T(8,128)S(1)}, u32[]{:S(2)}, u32[]{:S(2)}) collective-permute-start(f32[1,128,256]{2,1,0:T(8,128)S(1)} %get-tuple-element.52), channel_id=1, source_target_pairs={{0,1},{1,2},{2,3},{3,4},{4,5},{5,6},{6,7},{7,8},{8,9},{9,10},{10,1... | collective-permute-start | bytes 393224 | tf_op jit(solution)/shard_map/ppermute | solution.py:16
  10.8 46.4 %collective-permute-start.1 = (f32[1,128,256]{2,1,0:T(8,128)S(1)}, f32[1,128,256]{2,1,0:T(8,128)}, u32[]{:S(2)}, u32[]{:S(2)}) collective-permute-start(f32[1,128,256]{2,1,0:T(8,128)S(1)} %get-tuple-element.51), channel_id=1, source_target_pairs={{1,0},{2,1},{3,2},{4,3},{5,4},{6,5},{7,6},{8,7},{9,8},{10,9},{11,1... | collective-permute-start | bytes 393224 | tf_op jit(solution)/shard_map/ppermute | solution.py:19
  12.1 47.0 %collective-permute-start.2 = (f32[1,128,256]{2,1,0:T(8,128)S(1)}, f32[1,128,256]{2,1,0:T(8,128)}, u32[]{:S(2)}, u32[]{:S(2)}) collective-permute-start(f32[1,128,256]{2,1,0:T(8,128)S(1)} %get-tuple-element.53), channel_id=1, source_target_pairs={{0,1},{1,2},{2,3},{3,4},{4,5},{5,6},{6,7},{7,8},{8,9},{9,10},{10,1... | collective-permute-start | bytes 393224 | tf_op jit(solution)/shard_map/ppermute | solution.py:16
  18.0 41.2 %collective-permute-start.3 = (f32[1,128,256]{2,1,0:T(8,128)S(1)}, f32[1,128,256]{2,1,0:T(8,128)S(1)}, u32[]{:S(2)}, u32[]{:S(2)}) collective-permute-start(f32[1,128,256]{2,1,0:T(8,128)S(1)} %get-tuple-element.54), channel_id=1, source_target_pairs={{1,0},{2,1},{3,2},{4,3},{5,4},{6,5},{7,6},{8,7},{9,8},{10,9},{11,1... | collective-permute-start | bytes 393224 | tf_op jit(solution)/shard_map/ppermute | solution.py:19
  27.5 25.6 %copy-start.14 = (s32[16]{0:T(128)S(1)}, s32[16]{0:T(128)}, u32[]{:S(2)}) copy-start(s32[16]{0:T(128)} %param.7) | copy-start | bytes 196
  59.1 2.0 copy-start.1
  59.1 2.0 copy-start.3
  63.4 4.1 %collective-permute-start.4 = (f32[1,128,256]{2,1,0:T(8,128)S(1)}, f32[1,128,256]{2,1,0:T(8,128)S(1)}, u32[]{:S(2)}, u32[]{:S(2)}) collective-permute-start(f32[1,128,256]{2,1,0:T(8,128)S(1)} %get-tuple-element.49), channel_id=1, source_target_pairs={{0,1},{1,2},{2,3},{3,4},{4,5},{5,6},{6,7},{7,8},{8,9},{9,10},{10,1... | collective-permute-start | bytes 393224 | tf_op jit(solution)/shard_map/ppermute | solution.py:16
  65.6 3.2 %collective-permute-start.5 = (f32[1,128,256]{2,1,0:T(8,128)S(1)}, f32[1,128,256]{2,1,0:T(8,128)S(1)}, u32[]{:S(2)}, u32[]{:S(2)}) collective-permute-start(f32[1,128,256]{2,1,0:T(8,128)S(1)} %get-tuple-element.50), channel_id=1, source_target_pairs={{1,0},{2,1},{3,2},{4,3},{5,4},{6,5},{7,6},{8,7},{9,8},{10,9},{11,1... | collective-permute-start | bytes 393224 | tf_op jit(solution)/shard_map/ppermute | solution.py:19
  67.5 1.4 copy-start.12
  70.0 10.6 %copy-start.15 = (u32[32]{0:T(128)S(1)}, u32[32]{0:T(128)}, u32[]{:S(2)}) copy-start(u32[32]{0:T(128)} %constant.395) | copy-start | bytes 388
  72.2 10.0 %copy-start.4 = (f32[1,128,256]{2,1,0:T(8,128)S(1)}, f32[1,128,256]{2,1,0:T(8,128)}, u32[]{:S(2)}) copy-start(f32[1,128,256]{2,1,0:T(8,128)} %copy-done.2) | copy-start | bytes 393220
  72.9 8.9 %collective-permute-start.6 = (f32[1,128,256]{2,1,0:T(8,128)}, f32[1,128,256]{2,1,0:T(8,128)S(1)}, u32[]{:S(2)}, u32[]{:S(2)}) collective-permute-start(f32[1,128,256]{2,1,0:T(8,128)} %get-tuple-element.47), channel_id=1, source_target_pairs={{0,1},{1,2},{2,3},{3,4},{4,5},{5,6},{6,7},{7,8},{8,9},{9,10},{10,1... | collective-permute-start | bytes 393224 | tf_op jit(solution)/shard_map/ppermute | solution.py:16
  77.9 4.0 %collective-permute-start.7 = (f32[1,128,256]{2,1,0:T(8,128)S(1)}, f32[1,128,256]{2,1,0:T(8,128)S(1)}, u32[]{:S(2)}, u32[]{:S(2)}) collective-permute-start(f32[1,128,256]{2,1,0:T(8,128)S(1)} %get-tuple-element.48), channel_id=1, source_target_pairs={{1,0},{2,1},{3,2},{4,3},{5,4},{6,5},{7,6},{8,7},{9,8},{10,9},{11,1... | collective-permute-start | bytes 393224 | tf_op jit(solution)/shard_map/ppermute | solution.py:19
  82.2 2.7 %copy-start.16 = (s32[4]{0:T(128)S(1)}, s32[4]{0:T(128)}, u32[]{:S(2)}) copy-start(s32[4]{0:T(128)} %get-tuple-element.114) | copy-start | bytes 52
  82.3 2.7 %copy-start.17 = (s32[4]{0:T(128)S(1)}, s32[4]{0:T(128)}, u32[]{:S(2)}) copy-start(s32[4]{0:T(128)} %get-tuple-element.115) | copy-start | bytes 52
  85.3 113.4 %copy-start.5 = (f32[16,1984]{1,0:T(8,128)S(1)}, f32[16,1984]{1,0:T(8,128)}, u32[]{:S(2)}) copy-start(f32[16,1984]{1,0:T(8,128)} %get-tuple-element.99) | copy-start | bytes 380932
  85.4 113.4 %copy-start.6 = (f32[16,1984]{1,0:T(8,128)S(1)}, f32[16,1984]{1,0:T(8,128)}, u32[]{:S(2)}) copy-start(f32[16,1984]{1,0:T(8,128)} %get-tuple-element.100) | copy-start | bytes 380932
  85.4 113.4 %copy-start.7 = (f32[16,2047]{1,0:T(8,128)S(1)}, f32[16,2047]{1,0:T(8,128)}, u32[]{:S(2)}) copy-start(f32[16,2047]{1,0:T(8,128)} %get-tuple-element.97) | copy-start | bytes 393028
  85.4 113.4 %copy-start.8 = (f32[16,2047]{1,0:T(8,128)S(1)}, f32[16,2047]{1,0:T(8,128)}, u32[]{:S(2)}) copy-start(f32[16,2047]{1,0:T(8,128)} %get-tuple-element.98) | copy-start | bytes 393028
  85.4 113.4 %copy-start.9 = (f32[15,2048]{1,0:T(8,128)S(1)}, f32[15,2048]{1,0:T(8,128)}, u32[]{:S(2)}) copy-start(f32[15,2048]{1,0:T(8,128)} %get-tuple-element.122) | copy-start | bytes 368644
  85.4 113.4 %copy-start.10 = (f32[15,2048]{1,0:T(8,128)S(1)}, f32[15,2048]{1,0:T(8,128)}, u32[]{:S(2)}) copy-start(f32[15,2048]{1,0:T(8,128)} %get-tuple-element.123) | copy-start | bytes 368644
  (3 other events, 2.0 us)
Sparse Core Ops, SparseCore 0:
  86.7 87.3 all-reduce.61
where the time goes:
time: 213 us; the launch traced here: 212 us
  waiting for transfers between devices  88.9 us (42%)
  blocking collectives  46.4 us (22%)
  starting transfers between devices  20.6 us (10%)
  between operations  18.7 us (9%)
  local copies, waits for them, and re-layouts  16.8 us (8%)
  other arithmetic  15.6 us (7%)
  matrix products  5.18 us (2%)
    unnamed x2, waiting for transfers between devices  87.5 us
    all_gather x1, blocking collectives, local(): lax.all_gather(coarse_own, 'brick', axis=0, tiled=True)  23.8 us
    all_gather x1, blocking collectives, local(): lax.all_gather(held_rhs.reshape(cpd, cells), 'brick', axis=0, tiled=True)  22.6 us
    ppermute x4, starting transfers between devices, with_halo(): lax.ppermute(lax.slice_in_dim(block, block.shape[dim] - width, None, axis...  15.4 us
    reduce_sum x1, local copies, waits for them, and re-layouts, local(): perm.reshape(cpd, 4, cyc, 4, czc, 4).sum(axis=(1, 3, 5)) * (1.0 / 64.0)  5.67 us
    ppermute x4, starting transfers between devices, with_halo(): lax.ppermute(lax.slice_in_dim(block, 0, width, axis=dim), axis, backward)  5.16 us
    add x2, other arithmetic, local(): smooth = smooth + relax_weight * (source - image) / diagonal  4.4 us
  transfers between devices with their start and end apart: 9, of which 2 were waited for; matrix products, arithmetic and copies ran while one was open for 7% of the time, Pallas kernels for 0%

commit v1 on v0

--- a/solution.py
+++ b/solution.py
@@ -1,3 +1,4 @@
+import functools
 import jax
 import jax.numpy as jnp
 from jax import lax
@@ -6,6 +7,28 @@
 NU = 2
 SWEEPS = 8
 relax_weight = 0.8
+
+
+def replace_trails(values, axis_id):
+    response, opened, x_now = (lax.axis_size(axis_id), lax.axis_index(axis_id), values.shape[0])
+    nodes = [(dev, (dev + 1) % response) for dev in range(response)]
+    made = [(dev, (dev - 1) % response) for dev in range(response)]
+    z = jnp.zeros((*values.shape[:0], response * x_now, *values.shape[1:]), values.dtype)
+    z = lax.dynamic_update_slice_in_dim(z, values, opened * x_now, axis=0)
+    arr_out = base_arr = values
+    local_part = response // 2
+    for p in range(1, local_part + 1):
+        arr_out = lax.ppermute(arr_out, axis_id, nodes)
+        z = lax.dynamic_update_slice_in_dim(z, arr_out, (opened - p) % response * x_now, axis=0)
+        if p < response - local_part:
+            base_arr = lax.ppermute(base_arr, axis_id, made)
+            z = lax.dynamic_update_slice_in_dim(
+                z, base_arr, (opened + p) % response * x_now, axis=0
+            )
+    return z
+
+
+get_the_weights = functools.partial(replace_trails, axis_id="brick")
 
 
 def with_halo(block, sides, width):
@@ -147,7 +170,7 @@
     buffer = buffer + jnp.where((block_ids == next_dest) & has_next, upper_part[None], 0.0)
     held_rhs = lax.psum_scatter(buffer, "brick", scatter_dimension=0, tiled=True)
     gathered_rhs, coarse_perm = (
-        lax.all_gather(held_rhs.reshape(cpd, cells), "brick", axis=0, tiled=True),
+        get_the_weights(held_rhs.reshape(cpd, cells)),
         lax.all_gather(coarse_own, "brick", axis=0, tiled=True),
     )
     coarse_rhs = jnp.take(gathered_rhs.reshape(count, cpd, cells), owner, axis=0).reshape(

time: 213 us -> 228 us (1.070)
  starting transfers between devices: 20.6 us -> 53.6 us
  blocking collectives: 46.4 us -> 23.1 us
  waiting for transfers between devices: 88.9 us -> 95.8 us
    ppermute x0 -> x15, starting transfers between devices: none -> 31 us  [the longest x7 30.6 us: replace_trails(): base_arr = lax.ppermute(base_arr, axis_id, made)]
    all_gather x1 -> x0, blocking collectives: 22.6 us -> none  [local(): lax.all_gather(held_rhs.reshape(cpd, cells), 'brick', axis=0, tiled=True)]
    ppermute x0 -> x15, waiting for transfers between devices: none -> 8.71 us  [the longest x8 6.57 us: replace_trails(): arr_out = lax.ppermute(arr_out, axis_id, nodes)]
    dynamic_update_slice x0 -> x18, local copies, waits for them, and re-layouts: none -> 4.77 us  [the longest x10 3.13 us: replace_trails(): lax.dynamic_update_slice_in_dim(z, arr_out, (opened - p) % response * x_n...]
    unnamed x2, waiting for transfers between devices: 87.5 us -> 84 us
  transfers between devices with their start and end apart: 9 -> 24, of which waited for: 2 -> 15; matrix products, arithmetic and copies ran while one was open for 7% -> 7% of each run, Pallas kernels for 0% -> 0%
where the time goes in v1:
time: 228 us; the launch traced here: 227 us
  waiting for transfers between devices  95.8 us (42%)
  starting transfers between devices  53.6 us (24%)
  blocking collectives  23.1 us (10%)
  between operations  18.9 us (8%)
  local copies, waits for them, and re-layouts  17 us (7%)
  other arithmetic  14.3 us (6%)
  matrix products  4.28 us (2%)
    unnamed x2, waiting for transfers between devices  84 us
    ppermute x7, starting transfers between devices, replace_trails(): base_arr = lax.ppermute(base_arr, axis_id, made)  30.6 us
    all_gather x1, blocking collectives, local(): lax.all_gather(coarse_own, 'brick', axis=0, tiled=True)  23.1 us
    ppermute x4, starting transfers between devices, with_halo(): lax.ppermute(lax.slice_in_dim(block, block.shape[dim] - width, None, axis...  17.4 us
    ppermute x8, waiting for transfers between devices, replace_trails(): arr_out = lax.ppermute(arr_out, axis_id, nodes)  6.57 us
    reduce_sum x1, local copies, waits for them, and re-layouts, local(): perm.reshape(cpd, 4, cyc, 4, czc, 4).sum(axis=(1, 3, 5)) * (1.0 / 64.0)  5.7 us
    ppermute x4, starting transfers between devices, with_halo(): lax.ppermute(lax.slice_in_dim(block, 0, width, axis=dim), axis, backward)  5.16 us
  transfers between devices with their start and end apart: 24, of which 15 were waited for; matrix products, arithmetic and copies ran while one was open for 7% of the time, Pallas kernels for 0%

profile of v1, /device:TPU:0, one launch (start us, length us, event | category | flops | bytes accessed | tf_op | source)
XLA Modules:
  0.0 227.0 jit_solution(10426810684633416479)
XLA Ops:
  8.4 2.4 %collective-permute-start = (f32[1,128,256]{2,1,0:T(8,128)S(1)}, f32[1,128,256]{2,1,0:T(8,128)S(1)}, u32[]{:S(2)}, u32[]{:S(2)}) collective-permute-start(f32[1,128,256]{2,1,0:T(8,128)S(1)} %get-tuple-element.52), channel_id=1, source_target_pairs={{0,1},{1,2},{2,3},{3,4},{4,5},{5,6},{6,7},{7,8},{8,9},{9,10},{10,1... | collective-permute-start | bytes 393224 | tf_op jit(solution)/shard_map/ppermute | solution.py:39
  10.8 1.3 collective-permute-start.1
  12.8 5.8 %collective-permute-start.2 = (f32[1,128,256]{2,1,0:T(8,128)}, f32[1,128,256]{2,1,0:T(8,128)}, u32[]{:S(2)}, u32[]{:S(2)}) collective-permute-start(f32[1,128,256]{2,1,0:T(8,128)} %get-tuple-element.53), channel_id=1, source_target_pairs={{0,1},{1,2},{2,3},{3,4},{4,5},{5,6},{6,7},{7,8},{8,9},{9,10},{10,1... | collective-permute-start | bytes 393224 | tf_op jit(solution)/shard_map/ppermute | solution.py:39
  20.0 5.7 %reduce_sum.26 = f32[32,4,64,4]{3,2,1,0:T(8,128)} reshape(f32[128,256]{1,0:T(8,128)S(1)} %get-tuple-element.45) | data formatting | bytes 262144 | tf_op jit(solution)/shard_map/reduce_sum | solution.py:156
  25.7 2.6 %reduce_sum.27 = f32[32,64]{1,0:T(8,128)S(1)} reduce(f32[32,4,64,4]{3,2,1,0:T(8,128)} %reduce_sum.26, f32[]{:T(128)} %constant.278.clone.1), dimensions={1,3}, to_apply=%region_2.3 | reduce | flops 30720 | bytes 139268 | tf_op jit(solution)/shard_map/reduce_sum | solution.py:156
  31.6 1.4 select_maximum_fusion.4
  33.0 2.2 fusion.37
  35.2 3.6 %collective-permute-start.4 = (f32[1,128,256]{2,1,0:T(8,128)S(1)}, f32[1,128,256]{2,1,0:T(8,128)S(1)}, u32[]{:S(2)}, u32[]{:S(2)}) collective-permute-start(f32[1,128,256]{2,1,0:T(8,128)S(1)} %get-tuple-element.49), channel_id=1, source_target_pairs={{0,1},{1,2},{2,3},{3,4},{4,5},{5,6},{6,7},{7,8},{8,9},{9,10},{10,1... | collective-permute-start | bytes 393224 | tf_op jit(solution)/shard_map/ppermute | solution.py:39
  38.9 1.3 collective-permute-start.5
  40.3 3.0 %collective-permute-done.5 = f32[1,128,256]{2,1,0:T(8,128)S(1)} collective-permute-done((f32[1,128,256]{2,1,0:T(8,128)S(1)}, f32[1,128,256]{2,1,0:T(8,128)S(1)}, u32[]{:S(2)}, u32[]{:S(2)}) %collective-permute-start.5) | collective-permute-done | bytes 131104 | tf_op jit(solution)/shard_map/ppermute | solution.py:42
  44.4 2.2 fusion.25
  46.7 5.6 %collective-permute-start.6 = (f32[1,128,256]{2,1,0:T(8,128)S(1)}, f32[1,128,256]{2,1,0:T(8,128)S(1)}, u32[]{:S(2)}, u32[]{:S(2)}) collective-permute-start(f32[1,128,256]{2,1,0:T(8,128)S(1)} %get-tuple-element.47), channel_id=1, source_target_pairs={{0,1},{1,2},{2,3},{3,4},{4,5},{5,6},{6,7},{7,8},{8,9},{9,10},{10,1... | collective-permute-start | bytes 393224 | tf_op jit(solution)/shard_map/ppermute | solution.py:39
  53.6 23.1 %all-gather = f32[16,1,2048]{2,1,0:T(1,128)S(1)} all-gather(f32[1,1,2048]{2,1,0:T(1,128)S(1)} %reshape.704), channel_id=1, replica_groups=mesh['samples'=2,'brick'=16] {'brick'}, dimensions={0}, use_global_device_ids=true | all-gather | bytes 139264 | tf_op jit(solution)/shard_map/all_gather | solution.py:174
  77.1 1.5 convolution_bitcast_fusion
  81.3 84.0 %all-reduce.62.cloned.1.call-done = f32[16,1,2048]{2,1,0:T(1,128)} async-done(((f32[16,1,2048]{2,1,0:T(1,128)}), f32[16,1,2048]{2,1,0:T(1,128)}) %all-reduce.62.cloned.1.call-update) | async-done | bytes 131088
  165.4 1.3 dynamic-slice_bitcast_fusion
  167.2 4.2 %collective-permute-start.9 = (f32[1,2048]{1,0:T(1,128)S(1)}, f32[1,2048]{1,0:T(1,128)S(1)}, u32[]{:S(2)}, u32[]{:S(2)}) collective-permute-start(f32[1,2048]{1,0:T(1,128)S(1)} %dynamic-slice_bitcast_fusion), channel_id=1, source_target_pairs={{0,15},{1,0},{2,1},{3,2},{4,3},{5,4},{6,5},{7,6},{8,7},{9,8},{10,9... | collective-permute-start | bytes 24584 | tf_op jit(solution)/shard_map/ppermute | solution.py:24
  172.7 4.4 %collective-permute-start.11 = (f32[1,2048]{1,0:T(1,128)S(1)}, f32[1,2048]{1,0:T(1,128)S(1)}, u32[]{:S(2)}, u32[]{:S(2)}) collective-permute-start(f32[1,2048]{1,0:T(1,128)S(1)} %collective-permute-done.9), channel_id=1, source_target_pairs={{0,15},{1,0},{2,1},{3,2},{4,3},{5,4},{6,5},{7,6},{8,7},{9,8},{10,9... | collective-permute-start | bytes 24584 | tf_op jit(solution)/shard_map/ppermute | solution.py:24
  178.5 4.4 %collective-permute-start.13 = (f32[1,2048]{1,0:T(1,128)S(1)}, f32[1,2048]{1,0:T(1,128)S(1)}, u32[]{:S(2)}, u32[]{:S(2)}) collective-permute-start(f32[1,2048]{1,0:T(1,128)S(1)} %collective-permute-done.11), channel_id=1, source_target_pairs={{0,15},{1,0},{2,1},{3,2},{4,3},{5,4},{6,5},{7,6},{8,7},{9,8},{10,9... | collective-permute-start | bytes 24584 | tf_op jit(solution)/shard_map/ppermute | solution.py:24
  184.7 4.4 %collective-permute-start.15 = (f32[1,2048]{1,0:T(1,128)S(1)}, f32[1,2048]{1,0:T(1,128)S(1)}, u32[]{:S(2)}, u32[]{:S(2)}) collective-permute-start(f32[1,2048]{1,0:T(1,128)S(1)} %collective-permute-done.13), channel_id=1, source_target_pairs={{0,15},{1,0},{2,1},{3,2},{4,3},{5,4},{6,5},{7,6},{8,7},{9,8},{10,9... | collective-permute-start | bytes 24584 | tf_op jit(solution)/shard_map/ppermute | solution.py:24
  190.5 4.4 %collective-permute-start.17 = (f32[1,2048]{1,0:T(1,128)S(1)}, f32[1,2048]{1,0:T(1,128)S(1)}, u32[]{:S(2)}, u32[]{:S(2)}) collective-permute-start(f32[1,2048]{1,0:T(1,128)S(1)} %collective-permute-done.15), channel_id=1, source_target_pairs={{0,15},{1,0},{2,1},{3,2},{4,3},{5,4},{6,5},{7,6},{8,7},{9,8},{10,9... | collective-permute-start | bytes 24584 | tf_op jit(solution)/shard_map/ppermute | solution.py:24
  196.3 4.4 %collective-permute-start.19 = (f32[1,2048]{1,0:T(1,128)S(1)}, f32[1,2048]{1,0:T(1,128)S(1)}, u32[]{:S(2)}, u32[]{:S(2)}) collective-permute-start(f32[1,2048]{1,0:T(1,128)S(1)} %collective-permute-done.17), channel_id=1, source_target_pairs={{0,15},{1,0},{2,1},{3,2},{4,3},{5,4},{6,5},{7,6},{8,7},{9,8},{10,9... | collective-permute-start | bytes 24584 | tf_op jit(solution)/shard_map/ppermute | solution.py:24
  202.0 4.4 %collective-permute-start.21 = (f32[1,2048]{1,0:T(1,128)S(1)}, f32[1,2048]{1,0:T(1,128)S(1)}, u32[]{:S(2)}, u32[]{:S(2)}) collective-permute-start(f32[1,2048]{1,0:T(1,128)S(1)} %collective-permute-done.19), channel_id=1, source_target_pairs={{0,15},{1,0},{2,1},{3,2},{4,3},{5,4},{6,5},{7,6},{8,7},{9,8},{10,9... | collective-permute-start | bytes 24584 | tf_op jit(solution)/shard_map/ppermute | solution.py:24
  218.2 1.4 convolution_add_fusion
  (141 shorter events, 29.1 us)
Async XLA Ops:
  7.2 158.2 %all-reduce.62.cloned.1.call-start = ((), (), s32[]{:S(2)}) async-start(), calls=%async_computation | async-start | bytes 262144
  8.4 22.5 %collective-permute-start = (f32[1,128,256]{2,1,0:T(8,128)S(1)}, f32[1,128,256]{2,1,0:T(8,128)S(1)}, u32[]{:S(2)}, u32[]{:S(2)}) collective-permute-start(f32[1,128,256]{2,1,0:T(8,128)S(1)} %get-tuple-element.52), channel_id=1, source_target_pairs={{0,1},{1,2},{2,3},{3,4},{4,5},{5,6},{6,7},{7,8},{8,9},{9,10},{10,1... | collective-permute-start | bytes 393224 | tf_op jit(solution)/shard_map/ppermute | solution.py:39
  10.8 20.2 %collective-permute-start.1 = (f32[1,128,256]{2,1,0:T(8,128)S(1)}, f32[1,128,256]{2,1,0:T(8,128)S(1)}, u32[]{:S(2)}, u32[]{:S(2)}) collective-permute-start(f32[1,128,256]{2,1,0:T(8,128)S(1)} %get-tuple-element.51), channel_id=1, source_target_pairs={{1,0},{2,1},{3,2},{4,3},{5,4},{6,5},{7,6},{8,7},{9,8},{10,9},{11,1... | collective-permute-start | bytes 393224 | tf_op jit(solution)/shard_map/ppermute | solution.py:42
  12.8 18.6 %collective-permute-start.2 = (f32[1,128,256]{2,1,0:T(8,128)}, f32[1,128,256]{2,1,0:T(8,128)}, u32[]{:S(2)}, u32[]{:S(2)}) collective-permute-start(f32[1,128,256]{2,1,0:T(8,128)} %get-tuple-element.53), channel_id=1, source_target_pairs={{0,1},{1,2},{2,3},{3,4},{4,5},{5,6},{6,7},{7,8},{8,9},{9,10},{10,1... | collective-permute-start | bytes 393224 | tf_op jit(solution)/shard_map/ppermute | solution.py:39
  18.6 12.8 %collective-permute-start.3 = (f32[1,128,256]{2,1,0:T(8,128)}, f32[1,128,256]{2,1,0:T(8,128)}, u32[]{:S(2)}, u32[]{:S(2)}) collective-permute-start(f32[1,128,256]{2,1,0:T(8,128)} %get-tuple-element.54), channel_id=1, source_target_pairs={{1,0},{2,1},{3,2},{4,3},{5,4},{6,5},{7,6},{8,7},{9,8},{10,9},{11,1... | collective-permute-start | bytes 393224 | tf_op jit(solution)/shard_map/ppermute | solution.py:42
  35.2 5.1 %collective-permute-start.4 = (f32[1,128,256]{2,1,0:T(8,128)S(1)}, f32[1,128,256]{2,1,0:T(8,128)S(1)}, u32[]{:S(2)}, u32[]{:S(2)}) collective-permute-start(f32[1,128,256]{2,1,0:T(8,128)S(1)} %get-tuple-element.49), channel_id=1, source_target_pairs={{0,1},{1,2},{2,3},{3,4},{4,5},{5,6},{6,7},{7,8},{8,9},{9,10},{10,1... | collective-permute-start | bytes 393224 | tf_op jit(solution)/shard_map/ppermute | solution.py:39
  38.9 4.5 %collective-permute-start.5 = (f32[1,128,256]{2,1,0:T(8,128)S(1)}, f32[1,128,256]{2,1,0:T(8,128)S(1)}, u32[]{:S(2)}, u32[]{:S(2)}) collective-permute-start(f32[1,128,256]{2,1,0:T(8,128)S(1)} %get-tuple-element.50), channel_id=1, source_target_pairs={{1,0},{2,1},{3,2},{4,3},{5,4},{6,5},{7,6},{8,7},{9,8},{10,9},{11,1... | collective-permute-start | bytes 393224 | tf_op jit(solution)/shard_map/ppermute | solution.py:42
  46.7 30.0 %collective-permute-start.6 = (f32[1,128,256]{2,1,0:T(8,128)S(1)}, f32[1,128,256]{2,1,0:T(8,128)S(1)}, u32[]{:S(2)}, u32[]{:S(2)}) collective-permute-start(f32[1,128,256]{2,1,0:T(8,128)S(1)} %get-tuple-element.47), channel_id=1, source_target_pairs={{0,1},{1,2},{2,3},{3,4},{4,5},{5,6},{6,7},{7,8},{8,9},{9,10},{10,1... | collective-permute-start | bytes 393224 | tf_op jit(solution)/shard_map/ppermute | solution.py:39
  52.3 24.4 %collective-permute-start.7 = (f32[1,128,256]{2,1,0:T(8,128)S(1)}, f32[1,128,256]{2,1,0:T(8,128)S(1)}, u32[]{:S(2)}, u32[]{:S(2)}) collective-permute-start(f32[1,128,256]{2,1,0:T(8,128)S(1)} %get-tuple-element.48), channel_id=1, source_target_pairs={{1,0},{2,1},{3,2},{4,3},{5,4},{6,5},{7,6},{8,7},{9,8},{10,9},{11,1... | collective-permute-start | bytes 393224 | tf_op jit(solution)/shard_map/ppermute | solution.py:42
  166.7 5.8 %collective-permute-start.8 = (f32[1,2048]{1,0:T(1,128)S(1)}, f32[1,2048]{1,0:T(1,128)S(1)}, u32[]{:S(2)}, u32[]{:S(2)}) collective-permute-start(f32[1,2048]{1,0:T(1,128)S(1)} %dynamic-slice_bitcast_fusion), channel_id=1, source_target_pairs={{0,1},{1,2},{2,3},{3,4},{4,5},{5,6},{6,7},{7,8},{8,9},{9,10},{10,1... | collective-permute-start | bytes 24584 | tf_op jit(solution)/shard_map/ppermute | solution.py:21
  167.2 5.5 %collective-permute-start.9 = (f32[1,2048]{1,0:T(1,128)S(1)}, f32[1,2048]{1,0:T(1,128)S(1)}, u32[]{:S(2)}, u32[]{:S(2)}) collective-permute-start(f32[1,2048]{1,0:T(1,128)S(1)} %dynamic-slice_bitcast_fusion), channel_id=1, source_target_pairs={{0,15},{1,0},{2,1},{3,2},{4,3},{5,4},{6,5},{7,6},{8,7},{9,8},{10,9... | collective-permute-start | bytes 24584 | tf_op jit(solution)/shard_map/ppermute | solution.py:24
  172.5 5.8 %collective-permute-start.10 = (f32[1,2048]{1,0:T(1,128)S(1)}, f32[1,2048]{1,0:T(1,128)S(1)}, u32[]{:S(2)}, u32[]{:S(2)}) collective-permute-start(f32[1,2048]{1,0:T(1,128)S(1)} %collective-permute-done.8), channel_id=1, source_target_pairs={{0,1},{1,2},{2,3},{3,4},{4,5},{5,6},{6,7},{7,8},{8,9},{9,10},{10,1... | collective-permute-start | bytes 24584 | tf_op jit(solution)/shard_map/ppermute | solution.py:21
  172.7 5.8 %collective-permute-start.11 = (f32[1,2048]{1,0:T(1,128)S(1)}, f32[1,2048]{1,0:T(1,128)S(1)}, u32[]{:S(2)}, u32[]{:S(2)}) collective-permute-start(f32[1,2048]{1,0:T(1,128)S(1)} %collective-permute-done.9), channel_id=1, source_target_pairs={{0,15},{1,0},{2,1},{3,2},{4,3},{5,4},{6,5},{7,6},{8,7},{9,8},{10,9... | collective-permute-start | bytes 24584 | tf_op jit(solution)/shard_map/ppermute | solution.py:24
  178.3 5.8 %collective-permute-start.12 = (f32[1,2048]{1,0:T(1,128)S(1)}, f32[1,2048]{1,0:T(1,128)S(1)}, u32[]{:S(2)}, u32[]{:S(2)}) collective-permute-start(f32[1,2048]{1,0:T(1,128)S(1)} %collective-permute-done.10), channel_id=1, source_target_pairs={{0,1},{1,2},{2,3},{3,4},{4,5},{5,6},{6,7},{7,8},{8,9},{9,10},{10,1... | collective-permute-start | bytes 24584 | tf_op jit(solution)/shard_map/ppermute | solution.py:21
  178.5 6.2 %collective-permute-start.13 = (f32[1,2048]{1,0:T(1,128)S(1)}, f32[1,2048]{1,0:T(1,128)S(1)}, u32[]{:S(2)}, u32[]{:S(2)}) collective-permute-start(f32[1,2048]{1,0:T(1,128)S(1)} %collective-permute-done.11), channel_id=1, source_target_pairs={{0,15},{1,0},{2,1},{3,2},{4,3},{5,4},{6,5},{7,6},{8,7},{9,8},{10,9... | collective-permute-start | bytes 24584 | tf_op jit(solution)/shard_map/ppermute | solution.py:24
  184.0 5.8 %collective-permute-start.14 = (f32[1,2048]{1,0:T(1,128)S(1)}, f32[1,2048]{1,0:T(1,128)S(1)}, u32[]{:S(2)}, u32[]{:S(2)}) collective-permute-start(f32[1,2048]{1,0:T(1,128)S(1)} %collective-permute-done.12), channel_id=1, source_target_pairs={{0,1},{1,2},{2,3},{3,4},{4,5},{5,6},{6,7},{7,8},{8,9},{9,10},{10,1... | collective-permute-start | bytes 24584 | tf_op jit(solution)/shard_map/ppermute | solution.py:21
  184.7 5.8 %collective-permute-start.15 = (f32[1,2048]{1,0:T(1,128)S(1)}, f32[1,2048]{1,0:T(1,128)S(1)}, u32[]{:S(2)}, u32[]{:S(2)}) collective-permute-start(f32[1,2048]{1,0:T(1,128)S(1)} %collective-permute-done.13), channel_id=1, source_target_pairs={{0,15},{1,0},{2,1},{3,2},{4,3},{5,4},{6,5},{7,6},{8,7},{9,8},{10,9... | collective-permute-start | bytes 24584 | tf_op jit(solution)/shard_map/ppermute | solution.py:24
  189.8 5.8 %collective-permute-start.16 = (f32[1,2048]{1,0:T(1,128)S(1)}, f32[1,2048]{1,0:T(1,128)S(1)}, u32[]{:S(2)}, u32[]{:S(2)}) collective-permute-start(f32[1,2048]{1,0:T(1,128)S(1)} %collective-permute-done.14), channel_id=1, source_target_pairs={{0,1},{1,2},{2,3},{3,4},{4,5},{5,6},{6,7},{7,8},{8,9},{9,10},{10,1... | collective-permute-start | bytes 24584 | tf_op jit(solution)/shard_map/ppermute | solution.py:21
  190.5 5.8 %collective-permute-start.17 = (f32[1,2048]{1,0:T(1,128)S(1)}, f32[1,2048]{1,0:T(1,128)S(1)}, u32[]{:S(2)}, u32[]{:S(2)}) collective-permute-start(f32[1,2048]{1,0:T(1,128)S(1)} %collective-permute-done.15), channel_id=1, source_target_pairs={{0,15},{1,0},{2,1},{3,2},{4,3},{5,4},{6,5},{7,6},{8,7},{9,8},{10,9... | collective-permute-start | bytes 24584 | tf_op jit(solution)/shard_map/ppermute | solution.py:24
  195.6 5.8 %collective-permute-start.18 = (f32[1,2048]{1,0:T(1,128)S(1)}, f32[1,2048]{1,0:T(1,128)S(1)}, u32[]{:S(2)}, u32[]{:S(2)}) collective-permute-start(f32[1,2048]{1,0:T(1,128)S(1)} %collective-permute-done.16), channel_id=1, source_target_pairs={{0,1},{1,2},{2,3},{3,4},{4,5},{5,6},{6,7},{7,8},{8,9},{9,10},{10,1... | collective-permute-start | bytes 24584 | tf_op jit(solution)/shard_map/ppermute | solution.py:21
  196.3 5.8 %collective-permute-start.19 = (f32[1,2048]{1,0:T(1,128)S(1)}, f32[1,2048]{1,0:T(1,128)S(1)}, u32[]{:S(2)}, u32[]{:S(2)}) collective-permute-start(f32[1,2048]{1,0:T(1,128)S(1)} %collective-permute-done.17), channel_id=1, source_target_pairs={{0,15},{1,0},{2,1},{3,2},{4,3},{5,4},{6,5},{7,6},{8,7},{9,8},{10,9... | collective-permute-start | bytes 24584 | tf_op jit(solution)/shard_map/ppermute | solution.py:24
  201.4 5.8 %collective-permute-start.20 = (f32[1,2048]{1,0:T(1,128)S(1)}, f32[1,2048]{1,0:T(1,128)S(1)}, u32[]{:S(2)}, u32[]{:S(2)}) collective-permute-start(f32[1,2048]{1,0:T(1,128)S(1)} %collective-permute-done.18), channel_id=1, source_target_pairs={{0,1},{1,2},{2,3},{3,4},{4,5},{5,6},{6,7},{7,8},{8,9},{9,10},{10,1... | collective-permute-start | bytes 24584 | tf_op jit(solution)/shard_map/ppermute | solution.py:21
  202.0 10.3 %collective-permute-start.21 = (f32[1,2048]{1,0:T(1,128)S(1)}, f32[1,2048]{1,0:T(1,128)S(1)}, u32[]{:S(2)}, u32[]{:S(2)}) collective-permute-start(f32[1,2048]{1,0:T(1,128)S(1)} %collective-permute-done.19), channel_id=1, source_target_pairs={{0,15},{1,0},{2,1},{3,2},{4,3},{5,4},{6,5},{7,6},{8,7},{9,8},{10,9... | collective-permute-start | bytes 24584 | tf_op jit(solution)/shard_map/ppermute | solution.py:24
  207.1 5.8 %collective-permute-start.22 = (f32[1,2048]{1,0:T(1,128)S(1)}, f32[1,2048]{1,0:T(1,128)S(1)}, u32[]{:S(2)}, u32[]{:S(2)}) collective-permute-start(f32[1,2048]{1,0:T(1,128)S(1)} %collective-permute-done.20), channel_id=1, source_target_pairs={{0,1},{1,2},{2,3},{3,4},{4,5},{5,6},{6,7},{7,8},{8,9},{9,10},{10,1... | collective-permute-start | bytes 24584 | tf_op jit(solution)/shard_map/ppermute | solution.py:21
  (8 other events, 46.2 us)
Sparse Core Ops, SparseCore 0:
  80.7 84.6 all-reduce.61
